TPU v7x, 128 devices: a whole 4x4x4 slice. The times are simulated.
128 devices in a mesh: dp: 16 (over x, y), red: 8 (over z, core).
Axes of the slice: x: 4, y: 4, z: 4, core: 2. Of those that a mesh axis runs over, the one named last changes fastest.
Arguments:
- frames: bfloat16 [2048, 48, 1536], P(('dp', 'red')), may hold values from -36 to 36
- cotangent: bfloat16 [2048, 48, 1536], P(('dp', 'red')), may hold values from -6 to 6
- w_in: bfloat16 [1536, 3072], P('red'), may hold values from -0.15625 to 0.15625
- kernel: float32 [31, 1536], replicated, may hold values from -1 to 1
- gain: float32 [1536], replicated, may hold values from 0.25 to 1.75
- lengths: int32 [2048], replicated, may hold values from 1 to 47, as said below
Outputs:
- module_output: bfloat16 [2048, 48, 1536], P(('dp', 'red'))
- frame_gradient: bfloat16 [2048, 48, 1536], P(('dp', 'red'))
- grad_w_in: float32 [1536, 3072], P('red')
- grad_kernel: float32 [31, 1536], replicated
- grad_gain: float32 [1536], replicated
Inputs may be any that keep to these rules, and one draw needn't show every extreme that they name: The slots of each device, in order, form 16 groups of 1 slots. The q-th slot of group j on the device with dp index i and red index r and the q-th slot of group j on the device with dp index (2 j + 1 - i) mod 16 and the same red index have lengths that sum to exactly 48. The slots of dp index 0 all hold at least three quarters of 48 frames, rounded up.
All inputs are finite; a program needn't handle non-finite values.
Results may differ from a plain program's by a relative error of at most 0.0054.
Values may be sent and summed in bfloat16 or wider, within the bound.
A program may use at most 128 MiB of HBM per device.

v0:
```python
import jax
import jax.numpy as jnp
from jax import lax
from jax.sharding import PartitionSpec as P

EPSILON = 1e-05


def normalize(widened_frames):
    center = widened_frames - jnp.mean(widened_frames, axis=-1, keepdims=True)
    inv_std = lax.rsqrt(jnp.mean(center * center, axis=-1, keepdims=True) + EPSILON)
    return (center * inv_std, inv_std)


def block_pass(frames, cotangent, valid_frame_mask, segment, weights, kernel, gain):
    row_count, length, model_width = frames.shape
    tap_count = kernel.shape[0]
    reach = tap_count // 2
    widened_frames = frames.astype(jnp.float32)
    normed, inv_std = normalize(widened_frames)
    scaled = (normed * gain).astype(jnp.bfloat16)
    flat_in = scaled.reshape(row_count * length, model_width)
    hidden = jnp.dot(flat_in, weights, preferred_element_type=jnp.float32)
    hidden = hidden.reshape(row_count, length, 2 * model_width)
    value_portion = hidden[..., :model_width]
    gate_sigmoid = jax.nn.sigmoid(hidden[..., model_width:])
    frame_validity = valid_frame_mask.astype(jnp.float32)[..., None]
    gated_linear_output = value_portion * gate_sigmoid * frame_validity
    padded = jnp.pad(gated_linear_output, ((0, 0), (reach, reach), (0, 0)))
    seg_pad = jnp.pad(segment, ((0, 0), (reach, reach)), constant_values=-1)
    convolved_frames = jnp.zeros_like(gated_linear_output)
    for offset in range(tap_count):
        window = padded[:, offset : offset + length]
        same_seg = (seg_pad[:, offset : offset + length] == segment).astype(jnp.float32)[..., None]
        convolved_frames = convolved_frames + kernel[offset] * (window * same_seg)
    swish_activation = jax.nn.sigmoid(convolved_frames)
    module_output = (
        (widened_frames + convolved_frames * swish_activation) * frame_validity
    ).astype(jnp.bfloat16)
    incoming_gradient = cotangent.astype(jnp.float32) * frame_validity
    grad_conv = incoming_gradient * (
        swish_activation * (1.0 + convolved_frames * (1.0 - swish_activation))
    )
    grad_pad = jnp.pad(grad_conv, ((0, 0), (reach, reach), (0, 0)))
    gated_linear_gradient = jnp.zeros_like(gated_linear_output)
    kernel_terms = []
    for offset in range(tap_count):
        window = padded[:, offset : offset + length]
        same_seg = (seg_pad[:, offset : offset + length] == segment).astype(jnp.float32)[..., None]
        kernel_terms.append(jnp.sum(grad_conv * window * same_seg, axis=(0, 1)))
        back_start = 2 * reach - offset
        back_same = (seg_pad[:, back_start : back_start + length] == segment).astype(jnp.float32)[
            ..., None
        ]
        gated_linear_gradient = gated_linear_gradient + kernel[offset] * (
            grad_pad[:, back_start : back_start + length] * back_same
        )
    gated_linear_gradient = gated_linear_gradient * frame_validity
    grad_hidden = jnp.concatenate(
        [
            gated_linear_gradient * gate_sigmoid,
            gated_linear_gradient * value_portion * gate_sigmoid * (1.0 - gate_sigmoid),
        ],
        axis=-1,
    ).astype(jnp.bfloat16)
    flat_grad = grad_hidden.reshape(row_count * length, 2 * model_width)
    grad_scaled = lax.dot_general(
        flat_grad, weights, (((1,), (1,)), ((), ())), preferred_element_type=jnp.float32
    )
    grad_scaled = grad_scaled.reshape(row_count, length, model_width)
    gain_term = jnp.sum(grad_scaled * normed, axis=(0, 1))
    grad_normed = grad_scaled * gain
    frame_gradient = incoming_gradient + inv_std * (
        grad_normed
        - jnp.mean(grad_normed, axis=-1, keepdims=True)
        - normed * jnp.mean(grad_normed * normed, axis=-1, keepdims=True)
    )
    frame_gradient = (frame_gradient * frame_validity).astype(jnp.bfloat16)
    return (module_output, frame_gradient, flat_in, flat_grad, jnp.stack(kernel_terms), gain_term)


def local(frames, cotangent, w_in, kernel, gain, lengths):
    dp_size = lax.axis_size("dp")
    red_size = lax.axis_size("red")
    dp_index = lax.axis_index("dp")
    red_index = lax.axis_index("red")
    local_utts, length, model_width = frames.shape
    weights = lax.all_gather(w_in, "red", axis=0, tiled=True)
    positions = jnp.arange(length, dtype=jnp.int32)
    by_owner = lengths.reshape(dp_size, red_size, local_utts)
    own_lengths = lax.dynamic_slice(by_owner, (dp_index, red_index, 0), (1, 1, local_utts)).reshape(
        local_utts
    )
    valid_frame_mask = positions[None, :] < own_lengths[:, None]
    segment = jnp.where(valid_frame_mask, 0, 1).astype(jnp.int32)
    module_output, frame_gradient, flat_in, flat_grad, kernel_part, gain_part = block_pass(
        frames, cotangent, valid_frame_mask, segment, weights, kernel, gain
    )
    grad_scale = lax.rsqrt(jnp.sum(lengths).astype(jnp.float32))
    block_rows = model_width // (dp_size * red_size)
    ordered = flat_in.reshape(-1, red_size, dp_size, block_rows)
    ordered = jnp.transpose(ordered, (0, 2, 1, 3)).reshape(-1, model_width)
    owned_rows = lax.psum_scatter(
        lax.dot_general(
            ordered, flat_grad, (((0,), (0,)), ((), ())), preferred_element_type=jnp.float32
        ),
        ("dp", "red"),
        scatter_dimension=0,
        tiled=True,
    )
    grad_weights = lax.all_gather(owned_rows, "dp", axis=0, tiled=True)
    kernel_total, gain_total = lax.psum((kernel_part, gain_part), ("dp", "red"))
    return (
        module_output,
        frame_gradient,
        grad_weights * grad_scale,
        kernel_total * grad_scale,
        gain_total * grad_scale,
    )


def solution(mesh):
    placed = (
        P(("dp", "red"), None, None),
        P(("dp", "red"), None, None),
        P("red", None),
        P(),
        P(),
        P(),
    )
    return jax.shard_map(
        local,
        mesh=mesh,
        in_specs=placed,
        out_specs=(
            P(("dp", "red"), None, None),
            P(("dp", "red"), None, None),
            P("red", None),
            P(),
            P(),
        ),
        check_vma=False,
    )
```

profile of v0, /device:TPU:1, one launch (start us, length us, event | category | flops | bytes accessed | tf_op | source)
XLA Modules:
  0.0 923.5 jit_solution(477016552205187638)
XLA Ops:
  14.4 8.3 copy.13
  22.7 10.7 %reshape_reshape.3 = bf16[768,8,16,12]{0,3,2,1:T(8,128)(2,1)} reshape(bf16[16,48,1536]{1,0,2:T(8,128)(2,1)} %copy.13) | data formatting | bytes 4718592 | tf_op jit(solution)/shard_map/reshape;reshape | solution.py:101
  43.8 23.9 %all-gather.4.cloned.1.call-done = bf16[1536,3072]{1,0:T(8,128)(2,1)} async-done(((bf16[192,3072]{1,0:T(8,128)(2,1)}), bf16[1536,3072]{1,0:T(8,128)(2,1)}) %all-gather.4.cloned.1.call-update) | async-done | bytes 9437200 | tf_op jit(solution)/shard_map/all_gather | solution.py:88
  67.7 10.8 %fusion.3 = f32[16,48,3072]{2,1,0:T(8,128)S(1)} fusion(bf16[16,48,1536]{2,1,0:T(8,128)(2,1)} %fusion.11, bf16[1536,3072]{1,0:T(8,128)(2,1)} %all-gather.4.cloned.1.call-done), kind=kOutput, calls=%fused_computation.62 | convolution fusion | flops 7247757312 | bytes 21233664 | tf_op jit(solution)/shard_map/dot_general | solution.py:23
  82.6 49.2 %multiply_reduce_fusion = (f32[1536]{0:T(1024)}, f32[1536]{0:T(1024)}, f32[1536]{0:T(1024)}, f32[1536]{0:T(1024)}, f32[1536]{0:T(1024)}, /*index=5*/f32[1536]{0:...) fusion(f32[16,48,1536]{2,1,0:T(8,128)S(1)} %multiply_multiply_f, ...), kind=kLoop, calls=%fused_computation.186 | loop fusion | flops 150981120 | bytes 16856064 | tf_op jit(solution)/shard_map/reduce_sum | solution.py:50
  132.0 28.6 %multiply_convert_fusion.1 = (bf16[16,48,1536]{2,1,0:T(8,128)(2,1)S(1)}, f32[16,48,1536]{2,1,0:T(8,128)}) fusion(f32[16,48,3072]{2,1,0:T(8,128)} %copy-done.3, f32[16,48]{1,0:T(8,128)S(1)} %get-tuple-element.106, f32[16,48]{1,0:T(8,128)S(1)} %get-tuple-element.76, f32[1536]{0:T(1024)} %copy-done.57, f32[16,48]{1,0:T(8,128)S(1)} %get-tuple-element.77, ...), kind=kLoop, calls=%fused_computation.218 | loop fusion | flops 114425856 | bytes 16800768 | tf_op jit(solution)/shard_map/convert.4
  160.6 6.9 multiply_convert_fusion
  168.9 10.8 %fusion.119 = f32[1536,3072]{1,0:T(8,128)} fusion(bf16[768,1536]{0,1:T(8,128)(2,1)S(1)} %copy-done.8, bf16[768,1536]{1,0:T(8,128)(2,1)S(1)} %bitcast.24, bf16[768,1536]{1,0:T(8,128)(2,1)S(1)} %bitcast.23), kind=kOutput, calls=%fused_computation.182 | convolution fusion | flops 7257194496 | bytes 25952256 | tf_op jit(solution)/shard_map/dot_general | solution.py:104
  179.8 359.8 %fusion = f32[16,3072]{1,0:T(8,128)S(1)} fusion(f32[1536,3072]{1,0:T(8,128)} %fusion.119), kind=kCustom, calls=%all-reduce-scatter | all-reduce-scatter fusion | flops 6291457 | bytes 19070976
  552.0 15.3 %collective-permute-start.22 = (f32[16,3072]{1,0:T(8,128)S(1)}, f32[16,3072]{1,0:T(8,128)S(1)}, u32[]{:S(2)}, u32[]{:S(2)}) collective-permute-start(f32[16,3072]{1,0:T(8,128)S(1)} %fusion), channel_id=1, source_target_pairs={{0,23},{1,24},{2,25},{3,26},{4,27},{5,28},{6,29},{7,30},{8,31},{9,... | collective-permute-start | bytes 589832
  567.3 6.4 collective-permute-start.21
  579.4 8.4 collective-permute-start.19
  589.8 5.9 collective-permute-start.17
  608.6 12.3 %collective-permute-start.13 = (f32[16,3072]{1,0:T(8,128)S(1)}, f32[16,3072]{1,0:T(8,128)S(1)}, u32[]{:S(2)}, u32[]{:S(2)}) collective-permute-start(f32[16,3072]{1,0:T(8,128)S(1)} %fusion), channel_id=1, source_target_pairs={{0,14},{1,15},{2,16},{3,17},{4,18},{5,19},{6,20},{7,21},{8,22},{9,... | collective-permute-start | bytes 589832
  620.9 10.3 %collective-permute-start.12 = (f32[16,3072]{1,0:T(8,128)S(1)}, f32[16,3072]{1,0:T(8,128)S(1)}, u32[]{:S(2)}, u32[]{:S(2)}) collective-permute-start(f32[16,3072]{1,0:T(8,128)S(1)} %fusion), channel_id=1, source_target_pairs={{0,13},{1,14},{2,15},{3,16},{4,17},{5,18},{6,19},{7,20},{8,21},{9,... | collective-permute-start | bytes 589832
  631.2 14.7 %collective-permute-start.11 = (f32[16,3072]{1,0:T(8,128)S(1)}, f32[16,3072]{1,0:T(8,128)S(1)}, u32[]{:S(2)}, u32[]{:S(2)}) collective-permute-start(f32[16,3072]{1,0:T(8,128)S(1)} %fusion), channel_id=1, source_target_pairs={{0,12},{1,13},{2,14},{3,15},{4,16},{5,17},{6,18},{7,19},{8,20},{9,... | collective-permute-start | bytes 589832
  647.3 26.0 %multiply_reduce_fusion.9 = (f32[1536]{0:T(1024)S(1)}, f32[1536]{0:T(1024)S(1)}, f32[1536]{0:T(1024)S(1)}, f32[1536]{0:T(1024)S(1)}, f32[1536]{0:T(1024)S(1)}, /...) fusion(f32[16,48,1536]{2,1,0:T(8,128)} %copy-done.1, f32[16,48,1536]{2,1,0:T(8,128)} %copy-done, ...), kind=kLoop, calls=%fused_computation.195 | loop fusion | flops 30657024 | bytes 9517056 | tf_op jit(solution)/shard_map/reduce_sum | solution.py:50
  687.9 9.0 multiply_reduce_fusion.18
  697.0 6.7 collective-permute-start.4
  722.4 84.8 %concatenate.17 = f32[524,3072]{1,0:T(8,128)} concatenate(f32[12,3072]{1,0:T(8,128)S(1)} %collective-permute-done.31, f32[16,3072]{1,0:T(8,128)S(1)} %collective-permute-done.30, f32[16,3072]{1,0:T(8,128)} %copy-done.9, f32[16,3072]{1,0:T(8,128)} %copy-done.10, f32[16,3072]{1,0:T(8,128)} %copy-done.11, f32[16,3072]{1,0:T(8,128)} %copy-done.12, f32[16,3072]{1,0:T(8,128)} %copy-done.13, ...), dimensions={0} | concatenate | bytes 12877824
  808.9 14.3 %fusion.18 = (f32[1536]{0:T(1024)S(1)}, f32[16,48]{1,0:T(8,128)S(1)}, f32[16,48]{1,0:T(8,128)S(1)}, f32[16,48,1536]{2,1,0:T(8,128)}) fusion(bf16[16,48,1536]{2,1,0:T(8,128)(2,1)S(1)} %copy-done.4, f32[16,48]{1,0:T(8,128)S(1)} %copy-done.60, f32[16,48]{1,0:T(8,128)S(1)} %copy-done.52, f32[1536]{0:T(1024)S(1)} %copy-done.62, ...), kind=kOutput, calls=%fused_computation.80 | convolution fusion | flops 7267808256 | bytes 21258240 | tf_op jit(solution)/shard_map/dot_general | solution.py:67
  823.2 63.9 %psum.15 = f32[1536]{0:T(1024)S(1)} all-reduce(f32[1536]{0:T(1024)S(1)} %get-tuple-element.36), channel_id=1, replica_groups=mesh['dp'=16,'red'=8] {'dp','red'}, use_global_device_ids=true, to_apply=%region_39.40 | all-reduce | flops 1536 | bytes 12288 | tf_op jit(solution)/shard_map/psum | solution.py:112
  887.7 7.8 fusion.17
  897.2 12.9 %all-gather.6.cloned.1.call-done = f32[16,12,3072]{2,1,0:T(8,128)} async-done(((f32[1,12,3072]{2,1,0:T(8,128)}), f32[16,12,3072]{2,1,0:T(8,128)}) %all-gather.6.cloned.1.call-update) | async-done | bytes 2359312 | tf_op jit(solution)/shard_map/all_gather | solution.py:111
  (272 shorter events, 99.6 us)
Async XLA Ops:
  7.2 60.5 %all-gather.4.cloned.1.call-start = ((), (), s32[]{:S(2)}) async-start(), calls=%async_computation | async-start | bytes 10616832 | tf_op jit(solution)/shard_map/all_gather | solution.py:88
  7.9 887.6 %all-reduce.7.cloned.1.call-start = ((), (), s32[]{:S(2)}) async-start(), calls=%async_computation.1 | async-start | bytes 393216 | tf_op jit(solution)/shard_map/psum | solution.py:112
  547.5 26.2 %collective-permute-start.25 = (f32[16,3072]{1,0:T(8,128)S(1)}, f32[16,3072]{1,0:T(8,128)S(1)}, u32[]{:S(2)}, u32[]{:S(2)}) collective-permute-start(f32[16,3072]{1,0:T(8,128)S(1)} %fusion), channel_id=1, source_target_pairs={{0,26},{1,27},{2,28},{3,29},{4,30},{5,31},{6,32},{7,33},{8,34},{9,... | collective-permute-start | bytes 589832
  548.8 30.6 %collective-permute-start.24 = (f32[16,3072]{1,0:T(8,128)S(1)}, f32[16,3072]{1,0:T(8,128)S(1)}, u32[]{:S(2)}, u32[]{:S(2)}) collective-permute-start(f32[16,3072]{1,0:T(8,128)S(1)} %fusion), channel_id=1, source_target_pairs={{0,25},{1,26},{2,27},{3,28},{4,29},{5,30},{6,31},{7,32},{8,33},{9,... | collective-permute-start | bytes 589832
  550.2 37.6 %collective-permute-start.23 = (f32[16,3072]{1,0:T(8,128)S(1)}, f32[16,3072]{1,0:T(8,128)S(1)}, u32[]{:S(2)}, u32[]{:S(2)}) collective-permute-start(f32[16,3072]{1,0:T(8,128)S(1)} %fusion), channel_id=1, source_target_pairs={{0,24},{1,25},{2,26},{3,27},{4,28},{5,29},{6,30},{7,31},{8,32},{9,... | collective-permute-start | bytes 589832
  552.0 37.8 %collective-permute-start.22 = (f32[16,3072]{1,0:T(8,128)S(1)}, f32[16,3072]{1,0:T(8,128)S(1)}, u32[]{:S(2)}, u32[]{:S(2)}) collective-permute-start(f32[16,3072]{1,0:T(8,128)S(1)} %fusion), channel_id=1, source_target_pairs={{0,23},{1,24},{2,25},{3,26},{4,27},{5,28},{6,29},{7,30},{8,31},{9,... | collective-permute-start | bytes 589832
  567.3 28.4 %collective-permute-start.21 = (f32[16,3072]{1,0:T(8,128)S(1)}, f32[16,3072]{1,0:T(8,128)S(1)}, u32[]{:S(2)}, u32[]{:S(2)}) collective-permute-start(f32[16,3072]{1,0:T(8,128)S(1)} %fusion), channel_id=1, source_target_pairs={{0,22},{1,23},{2,24},{3,25},{4,26},{5,27},{6,28},{7,29},{8,30},{9,... | collective-permute-start | bytes 589832
  573.7 24.0 %collective-permute-start.20 = (f32[16,3072]{1,0:T(8,128)S(1)}, f32[16,3072]{1,0:T(8,128)S(1)}, u32[]{:S(2)}, u32[]{:S(2)}) collective-permute-start(f32[16,3072]{1,0:T(8,128)S(1)} %fusion), channel_id=1, source_target_pairs={{0,21},{1,22},{2,23},{3,24},{4,25},{5,26},{6,27},{7,28},{8,29},{9,... | collective-permute-start | bytes 589832
  579.4 23.7 %collective-permute-start.19 = (f32[16,3072]{1,0:T(8,128)S(1)}, f32[16,3072]{1,0:T(8,128)}, u32[]{:S(2)}, u32[]{:S(2)}) collective-permute-start(f32[16,3072]{1,0:T(8,128)S(1)} %fusion), channel_id=1, source_target_pairs={{0,20},{1,21},{2,22},{3,23},{4,24},{5,25},{6,26},{7,27},{8,28},{9,... | collective-permute-start | bytes 589832
  589.8 31.1 %collective-permute-start.17 = (f32[16,3072]{1,0:T(8,128)S(1)}, f32[16,3072]{1,0:T(8,128)}, u32[]{:S(2)}, u32[]{:S(2)}) collective-permute-start(f32[16,3072]{1,0:T(8,128)S(1)} %fusion), channel_id=1, source_target_pairs={{0,18},{1,19},{2,20},{3,21},{4,22},{5,23},{6,24},{7,25},{8,26},{9,... | collective-permute-start | bytes 589832
  595.7 35.5 %collective-permute-start.16 = (f32[16,3072]{1,0:T(8,128)S(1)}, f32[16,3072]{1,0:T(8,128)}, u32[]{:S(2)}, u32[]{:S(2)}) collective-permute-start(f32[16,3072]{1,0:T(8,128)S(1)} %fusion), channel_id=1, source_target_pairs={{0,17},{1,18},{2,19},{3,20},{4,21},{5,22},{6,23},{7,24},{8,25},{9,... | collective-permute-start | bytes 589832
  597.7 48.2 %collective-permute-start.15 = (f32[16,3072]{1,0:T(8,128)S(1)}, f32[16,3072]{1,0:T(8,128)}, u32[]{:S(2)}, u32[]{:S(2)}) collective-permute-start(f32[16,3072]{1,0:T(8,128)S(1)} %fusion), channel_id=1, source_target_pairs={{0,16},{1,17},{2,18},{3,19},{4,20},{5,21},{6,22},{7,23},{8,24},{9,... | collective-permute-start | bytes 589832
  603.1 70.1 %collective-permute-start.14 = (f32[16,3072]{1,0:T(8,128)S(1)}, f32[16,3072]{1,0:T(8,128)S(1)}, u32[]{:S(2)}, u32[]{:S(2)}) collective-permute-start(f32[16,3072]{1,0:T(8,128)S(1)} %fusion), channel_id=1, source_target_pairs={{0,15},{1,16},{2,17},{3,18},{4,19},{5,20},{6,21},{7,22},{8,23},{9,... | collective-permute-start | bytes 589832
  608.6 65.9 %collective-permute-start.13 = (f32[16,3072]{1,0:T(8,128)S(1)}, f32[16,3072]{1,0:T(8,128)S(1)}, u32[]{:S(2)}, u32[]{:S(2)}) collective-permute-start(f32[16,3072]{1,0:T(8,128)S(1)} %fusion), channel_id=1, source_target_pairs={{0,14},{1,15},{2,16},{3,17},{4,18},{5,19},{6,20},{7,21},{8,22},{9,... | collective-permute-start | bytes 589832
  620.9 58.9 %collective-permute-start.12 = (f32[16,3072]{1,0:T(8,128)S(1)}, f32[16,3072]{1,0:T(8,128)S(1)}, u32[]{:S(2)}, u32[]{:S(2)}) collective-permute-start(f32[16,3072]{1,0:T(8,128)S(1)} %fusion), channel_id=1, source_target_pairs={{0,13},{1,14},{2,15},{3,16},{4,17},{5,18},{6,19},{7,20},{8,21},{9,... | collective-permute-start | bytes 589832
  631.2 50.6 %collective-permute-start.11 = (f32[16,3072]{1,0:T(8,128)S(1)}, f32[16,3072]{1,0:T(8,128)S(1)}, u32[]{:S(2)}, u32[]{:S(2)}) collective-permute-start(f32[16,3072]{1,0:T(8,128)S(1)} %fusion), channel_id=1, source_target_pairs={{0,12},{1,13},{2,14},{3,15},{4,16},{5,17},{6,18},{7,19},{8,20},{9,... | collective-permute-start | bytes 589832
  646.0 38.4 %collective-permute-start.10 = (f32[16,3072]{1,0:T(8,128)S(1)}, f32[16,3072]{1,0:T(8,128)S(1)}, u32[]{:S(2)}, u32[]{:S(2)}) collective-permute-start(f32[16,3072]{1,0:T(8,128)S(1)} %fusion), channel_id=1, source_target_pairs={{0,11},{1,12},{2,13},{3,14},{4,15},{5,16},{6,17},{7,18},{8,19},{9,... | collective-permute-start | bytes 589832
  673.3 23.7 %collective-permute-start.9 = (f32[16,3072]{1,0:T(8,128)S(1)}, f32[16,3072]{1,0:T(8,128)S(1)}, u32[]{:S(2)}, u32[]{:S(2)}) collective-permute-start(f32[16,3072]{1,0:T(8,128)S(1)} %fusion), channel_id=1, source_target_pairs={{0,10},{1,11},{2,12},{3,13},{4,14},{5,15},{6,16},{7,17},{8,18},{9,... | collective-permute-start | bytes 589832
  674.6 29.1 %collective-permute-start.8 = (f32[16,3072]{1,0:T(8,128)S(1)}, f32[16,3072]{1,0:T(8,128)S(1)}, u32[]{:S(2)}, u32[]{:S(2)}) collective-permute-start(f32[16,3072]{1,0:T(8,128)S(1)} %fusion), channel_id=1, source_target_pairs={{0,9},{1,10},{2,11},{3,12},{4,13},{5,14},{6,15},{7,16},{8,17},{9,1... | collective-permute-start | bytes 589832
  679.9 25.8 %collective-permute-start.7 = (f32[16,3072]{1,0:T(8,128)S(1)}, f32[16,3072]{1,0:T(8,128)S(1)}, u32[]{:S(2)}, u32[]{:S(2)}) collective-permute-start(f32[16,3072]{1,0:T(8,128)S(1)} %fusion), channel_id=1, source_target_pairs={{0,8},{1,9},{2,10},{3,11},{4,12},{5,13},{6,14},{7,15},{8,16},{9,17... | collective-permute-start | bytes 589832
  681.8 28.5 %collective-permute-start.6 = (f32[16,3072]{1,0:T(8,128)S(1)}, f32[16,3072]{1,0:T(8,128)S(1)}, u32[]{:S(2)}, u32[]{:S(2)}) collective-permute-start(f32[16,3072]{1,0:T(8,128)S(1)} %fusion), channel_id=1, source_target_pairs={{0,7},{1,8},{2,9},{3,10},{4,11},{5,12},{6,13},{7,14},{8,15},{9,16}... | collective-permute-start | bytes 589832
  685.1 27.1 %collective-permute-start.5 = (f32[16,3072]{1,0:T(8,128)S(1)}, f32[16,3072]{1,0:T(8,128)S(1)}, u32[]{:S(2)}, u32[]{:S(2)}) collective-permute-start(f32[16,3072]{1,0:T(8,128)S(1)} %fusion), channel_id=1, source_target_pairs={{0,6},{1,7},{2,8},{3,9},{4,10},{5,11},{6,12},{7,13},{8,14},{9,15},... | collective-permute-start | bytes 589832
  697.0 25.4 %collective-permute-start.4 = (f32[16,3072]{1,0:T(8,128)S(1)}, f32[16,3072]{1,0:T(8,128)}, u32[]{:S(2)}, u32[]{:S(2)}) collective-permute-start(f32[16,3072]{1,0:T(8,128)S(1)} %fusion), channel_id=1, source_target_pairs={{0,5},{1,6},{2,7},{3,8},{4,9},{5,10},{6,11},{7,12},{8,13},{9,14},{... | collective-permute-start | bytes 589832
  722.3 187.8 %all-gather.6.cloned.1.call-start = ((), (), s32[]{:S(2)}) async-start(), calls=%async_computation.2 | async-start | bytes 3342336 | tf_op jit(solution)/shard_map/all_gather | solution.py:111
  (86 other events, 4127.2 us)
Sparse Core Ops, SparseCore 0:
  9.7 57.9 all-gather.3
  722.4 139.3 all-reduce.6
  864.2 45.8 all-gather.5
where the time goes:
time: 927 us; the launch traced here: 924 us
  blocking collectives  424 us (46%)
  other arithmetic  145 us (16%)
  starting transfers between devices  136 us (15%)
  local copies, waits for them, and re-layouts  128 us (14%)
  waiting for transfers between devices  38.2 us (4%)
  matrix products  35.9 us (4%)
  between operations  16.2 us (2%)
    unnamed x1, blocking collectives  360 us
    unnamed x32, starting transfers between devices  136 us
    unnamed x153, local copies, waits for them, and re-layouts  92.8 us
    reduce_sum x4, other arithmetic, block_pass(): kernel_terms.append(jnp.sum(grad_conv * window * same_seg, axis=(0, 1)))  88.1 us
    psum x1, blocking collectives, local(): kernel_total, gain_total = lax.psum((kernel_part, gain_part), ('dp', 'red'))  63.9 us
    another operation x2, other arithmetic  35.5 us
    all_gather x1, waiting for transfers between devices, local(): weights = lax.all_gather(w_in, 'red', axis=0, tiled=True)  23.9 us
  transfers between devices with their start and end apart: 35, of which 3 were waited for; matrix products, arithmetic and copies ran while one was open for 20% of the time, Pallas kernels for 0%

commit v1 on v0

--- a/solution.py
+++ b/solution.py
@@ -85,7 +85,8 @@
     dp_index = lax.axis_index("dp")
     red_index = lax.axis_index("red")
     local_utts, length, model_width = frames.shape
-    weights = lax.all_gather(w_in, "red", axis=0, tiled=True)
+    outgoing = jnp.stack([w_in] * lax.axis_size("red"))
+    weights = jnp.concatenate(lax.all_to_all(outgoing, "red", 0, 0), axis=0)
     positions = jnp.arange(length, dtype=jnp.int32)
     by_owner = lengths.reshape(dp_size, red_size, local_utts)
     own_lengths = lax.dynamic_slice(by_owner, (dp_index, red_index, 0), (1, 1, local_utts)).reshape(

time: 927 us -> 968 us (1.044)
  waiting for transfers between devices: 38.2 us -> 83.4 us
    all_to_all x0 -> x1, waiting for transfers between devices: none -> 72.3 us  [local(): weights = jnp.concatenate(lax.all_to_all(outgoing, 'red', 0, 0), axis=0)]
    all_gather x1 -> x0, waiting for transfers between devices: 23.9 us -> none  [local(): weights = lax.all_gather(w_in, 'red', axis=0, tiled=True)]
    all_gather x1, waiting for transfers between devices: 12.9 us -> 0.01 us  [local(): grad_weights = lax.all_gather(owned_rows, 'dp', axis=0, tiled=True)]
    unnamed x32, starting transfers between devices: 136 us -> 125 us
    unnamed x35 -> x34, waiting for transfers between devices: 1.34 us -> 11.1 us
    unnamed x153 -> x131, local copies, waits for them, and re-layouts: 92.8 us -> 92.7 us
  transfers between devices with their start and end apart: 35 -> 35, of which waited for: 3 -> 3; matrix products, arithmetic and copies ran while one was open for 20% -> 19% of each run, Pallas kernels for 0% -> 0%
where the time goes in v1:
time: 968 us; the launch traced here: 964 us
  blocking collectives  424 us (44%)
  other arithmetic  139 us (14%)
  local copies, waits for them, and re-layouts  132 us (14%)
  starting transfers between devices  132 us (14%)
  waiting for transfers between devices  83.4 us (9%)
  matrix products  35.9 us (4%)
  between operations  17.7 us (2%)
    unnamed x1, blocking collectives  360 us
    unnamed x32, starting transfers between devices  125 us
    unnamed x131, local copies, waits for them, and re-layouts  92.7 us
    reduce_sum x4, other arithmetic, block_pass(): kernel_terms.append(jnp.sum(grad_conv * window * same_seg, axis=(0, 1)))  87.3 us
    all_to_all x1, waiting for transfers between devices, local(): weights = jnp.concatenate(lax.all_to_all(outgoing, 'red', 0, 0), axis=0)  72.3 us
    psum x1, blocking collectives, local(): kernel_total, gain_total = lax.psum((kernel_part, gain_part), ('dp', 'red'))  63.9 us
    another operation x2, other arithmetic  34.1 us
  transfers between devices with their start and end apart: 35, of which 3 were waited for; matrix products, arithmetic and copies ran while one was open for 19% of the time, Pallas kernels for 0%

profile of v1, /device:TPU:1, one launch (start us, length us, event | category | flops | bytes accessed | tf_op | source)
XLA Modules:
  0.0 963.9 jit_solution(3489634678133733957)
XLA Ops:
  14.1 6.9 all-to-all-start
  25.1 8.3 copy.13
  33.4 10.5 %reshape_reshape.3 = bf16[768,8,16,12]{0,3,2,1:T(8,128)(2,1)} reshape(bf16[16,48,1536]{1,0,2:T(8,128)(2,1)} %copy.13) | data formatting | bytes 4718592 | tf_op jit(solution)/shard_map/reshape;reshape | solution.py:102
  53.8 72.3 %all-to-all-done = bf16[8,192,3072]{2,1,0:T(8,128)(2,1)} async-done(((bf16[8,192,3072]{2,1,0:T(8,128)(2,1)}), bf16[8,192,3072]{2,1,0:T(8,128)(2,1)}, u32[]{:S(2)}, u32[]{:S(2)}) %all-to-all-start) | async-done | bytes 9437216 | tf_op jit(solution)/shard_map/all_to_all | solution.py:89
  126.1 10.8 %fusion.155 = f32[16,48,3072]{2,1,0:T(8,128)S(1)} fusion(bf16[16,48,1536]{2,1,0:T(8,128)(2,1)} %fusion.7, bf16[1536,3072,1]{1,0,2:T(8,128)(2,1)} %bitcast.1), kind=kOutput, calls=%fused_computation.327 | convolution fusion | flops 7247757312 | bytes 21233664 | tf_op jit(solution)/shard_map/dot_general | solution.py:23
  140.9 48.5 %multiply_reduce_fusion = (f32[1536]{0:T(1024)}, f32[1536]{0:T(1024)}, f32[1536]{0:T(1024)}, f32[1536]{0:T(1024)}, f32[1536]{0:T(1024)}, /*index=5*/f32[1536]{0:...) fusion(f32[16,48,1536]{2,1,0:T(8,128)S(1)} %multiply_multiply_f, ...), kind=kLoop, calls=%fused_computation.183 | loop fusion | flops 150981120 | bytes 16856064 | tf_op jit(solution)/shard_map/reduce_sum | solution.py:50
  189.5 27.9 %multiply_convert_fusion.1 = (bf16[16,48,1536]{2,1,0:T(8,128)(2,1)}, f32[16,48,1536]{2,1,0:T(8,128)}) fusion(f32[16,48,3072]{2,1,0:T(8,128)} %copy-done.3, f32[16,48]{1,0:T(8,128)S(1)} %get-tuple-element.106, f32[16,48]{1,0:T(8,128)S(1)} %get-tuple-element.76, f32[1536]{0:T(1024)S(1)} %get-tuple-element.68, f32[16,48]{1,0:T(8,128)S(1)} %get-tuple-element.77, ...), kind=kLoop, calls=%fused_computation.215 | loop fusion | flops 114425856 | bytes 16800768 | tf_op jit(solution)/shard_map/convert.4
  217.4 6.2 multiply_convert_fusion
  225.0 10.8 %fusion.116 = f32[1536,3072]{1,0:T(8,128)} fusion(bf16[768,1536]{0,1:T(8,128)(2,1)S(1)} %copy-done.8, bf16[768,1536]{1,0:T(8,128)(2,1)S(1)} %bitcast.22, bf16[768,1536]{1,0:T(8,128)(2,1)S(1)} %bitcast.21), kind=kOutput, calls=%fused_computation.179 | convolution fusion | flops 7257194496 | bytes 25952256 | tf_op jit(solution)/shard_map/dot_general | solution.py:105
  235.9 360.4 %fusion = f32[16,3072]{1,0:T(8,128)S(1)} fusion(f32[1536,3072]{1,0:T(8,128)} %fusion.116), kind=kCustom, calls=%all-reduce-scatter | all-reduce-scatter fusion | flops 6291457 | bytes 19070976
  611.1 12.0 %collective-permute-start.22 = (f32[16,3072]{1,0:T(8,128)S(1)}, f32[16,3072]{1,0:T(8,128)S(1)}, u32[]{:S(2)}, u32[]{:S(2)}) collective-permute-start(f32[16,3072]{1,0:T(8,128)S(1)} %fusion), channel_id=1, source_target_pairs={{0,23},{1,24},{2,25},{3,26},{4,27},{5,28},{6,29},{7,30},{8,31},{9,... | collective-permute-start | bytes 589832
  623.1 6.4 collective-permute-start.21
  635.2 8.4 collective-permute-start.19
  645.6 8.1 collective-permute-done.22
  664.5 12.1 %collective-permute-start.13 = (f32[16,3072]{1,0:T(8,128)S(1)}, f32[16,3072]{1,0:T(8,128)S(1)}, u32[]{:S(2)}, u32[]{:S(2)}) collective-permute-start(f32[16,3072]{1,0:T(8,128)S(1)} %fusion), channel_id=1, source_target_pairs={{0,14},{1,15},{2,16},{3,17},{4,18},{5,19},{6,20},{7,21},{8,22},{9,... | collective-permute-start | bytes 589832
  676.7 10.3 %collective-permute-start.12 = (f32[16,3072]{1,0:T(8,128)S(1)}, f32[16,3072]{1,0:T(8,128)S(1)}, u32[]{:S(2)}, u32[]{:S(2)}) collective-permute-start(f32[16,3072]{1,0:T(8,128)S(1)} %fusion), channel_id=1, source_target_pairs={{0,13},{1,14},{2,15},{3,16},{4,17},{5,18},{6,19},{7,20},{8,21},{9,... | collective-permute-start | bytes 589832
  687.0 14.7 %collective-permute-start.11 = (f32[16,3072]{1,0:T(8,128)S(1)}, f32[16,3072]{1,0:T(8,128)S(1)}, u32[]{:S(2)}, u32[]{:S(2)}) collective-permute-start(f32[16,3072]{1,0:T(8,128)S(1)} %fusion), channel_id=1, source_target_pairs={{0,12},{1,13},{2,14},{3,15},{4,16},{5,17},{6,18},{7,19},{8,20},{9,... | collective-permute-start | bytes 589832
  703.0 25.9 %multiply_reduce_fusion.9 = (f32[1536]{0:T(1024)S(1)}, f32[1536]{0:T(1024)S(1)}, f32[1536]{0:T(1024)S(1)}, f32[1536]{0:T(1024)S(1)}, f32[1536]{0:T(1024)S(1)}, /...) fusion(f32[16,48,1536]{2,1,0:T(8,128)} %copy-done.1, f32[16,48,1536]{2,1,0:T(8,128)} %copy-done, ...), kind=kLoop, calls=%fused_computation.192 | loop fusion | flops 30657024 | bytes 9517056 | tf_op jit(solution)/shard_map/reduce_sum | solution.py:50
  743.6 9.0 multiply_reduce_fusion.18
  752.7 6.7 collective-permute-start.4
  778.1 84.8 %concatenate.17 = f32[524,3072]{1,0:T(8,128)} concatenate(f32[12,3072]{1,0:T(8,128)S(1)} %collective-permute-done.31, f32[16,3072]{1,0:T(8,128)S(1)} %collective-permute-done.30, f32[16,3072]{1,0:T(8,128)} %copy-done.9, f32[16,3072]{1,0:T(8,128)} %copy-done.10, f32[16,3072]{1,0:T(8,128)} %copy-done.11, f32[16,3072]{1,0:T(8,128)} %copy-done.12, f32[16,3072]{1,0:T(8,128)} %copy-done.13, ...), dimensions={0} | concatenate | bytes 12877824
  864.6 14.3 %fusion.14 = (f32[1536]{0:T(1024)S(1)}, f32[16,48]{1,0:T(8,128)S(1)}, f32[16,48]{1,0:T(8,128)S(1)}, f32[16,48,1536]{2,1,0:T(8,128)}) fusion(bf16[16,48,1536]{2,1,0:T(8,128)(2,1)S(1)} %copy-done.4, f32[16,48]{1,0:T(8,128)S(1)} %copy-done.49, f32[16,48]{1,0:T(8,128)S(1)} %copy-done.47, f32[1536]{0:T(1024)S(1)} %copy-done.51, ...), kind=kOutput, calls=%fused_computation.76 | convolution fusion | flops 7267808256 | bytes 21258240 | tf_op jit(solution)/shard_map/dot_general | solution.py:67
  878.9 63.9 %psum.15 = f32[1536]{0:T(1024)S(1)} all-reduce(f32[1536]{0:T(1024)S(1)} %get-tuple-element.36), channel_id=1, replica_groups=mesh['dp'=16,'red'=8] {'dp','red'}, use_global_device_ids=true, to_apply=%region_39.40 | all-reduce | flops 1536 | bytes 12288 | tf_op jit(solution)/shard_map/psum | solution.py:113
  943.3 7.8 fusion.13
  (250 shorter events, 99.3 us)
Async XLA Ops:
  14.1 112.0 %all-to-all-start = ((bf16[8,192,3072]{2,1,0:T(8,128)(2,1)}), bf16[8,192,3072]{2,1,0:T(8,128)(2,1)}, u32[]{:S(2)}, u32[]{:S(2)}) async-start(bf16[8,192,3072]{2,1,0:T(8,128)(2,1)} %stack.107), calls=%async_computation | async-start | bytes 18874368 | tf_op jit(solution)/shard_map/all_to_all | solution.py:89
  21.0 930.1 %all-reduce.7.cloned.1.call-start = ((), (), s32[]{:S(2)}) async-start(), calls=%async_computation.1 | async-start | bytes 393216 | tf_op jit(solution)/shard_map/psum | solution.py:113
  604.1 25.3 %collective-permute-start.25 = (f32[16,3072]{1,0:T(8,128)S(1)}, f32[16,3072]{1,0:T(8,128)S(1)}, u32[]{:S(2)}, u32[]{:S(2)}) collective-permute-start(f32[16,3072]{1,0:T(8,128)S(1)} %fusion), channel_id=1, source_target_pairs={{0,26},{1,27},{2,28},{3,29},{4,30},{5,31},{6,32},{7,33},{8,34},{9,... | collective-permute-start | bytes 589832
  605.5 29.7 %collective-permute-start.24 = (f32[16,3072]{1,0:T(8,128)S(1)}, f32[16,3072]{1,0:T(8,128)S(1)}, u32[]{:S(2)}, u32[]{:S(2)}) collective-permute-start(f32[16,3072]{1,0:T(8,128)S(1)} %fusion), channel_id=1, source_target_pairs={{0,25},{1,26},{2,27},{3,28},{4,29},{5,30},{6,31},{7,32},{8,33},{9,... | collective-permute-start | bytes 589832
  606.8 36.8 %collective-permute-start.23 = (f32[16,3072]{1,0:T(8,128)S(1)}, f32[16,3072]{1,0:T(8,128)S(1)}, u32[]{:S(2)}, u32[]{:S(2)}) collective-permute-start(f32[16,3072]{1,0:T(8,128)S(1)} %fusion), channel_id=1, source_target_pairs={{0,24},{1,25},{2,26},{3,27},{4,28},{5,29},{6,30},{7,31},{8,32},{9,... | collective-permute-start | bytes 589832
  611.1 42.6 %collective-permute-start.22 = (f32[16,3072]{1,0:T(8,128)S(1)}, f32[16,3072]{1,0:T(8,128)S(1)}, u32[]{:S(2)}, u32[]{:S(2)}) collective-permute-start(f32[16,3072]{1,0:T(8,128)S(1)} %fusion), channel_id=1, source_target_pairs={{0,23},{1,24},{2,25},{3,26},{4,27},{5,28},{6,29},{7,30},{8,31},{9,... | collective-permute-start | bytes 589832
  623.1 32.5 %collective-permute-start.21 = (f32[16,3072]{1,0:T(8,128)S(1)}, f32[16,3072]{1,0:T(8,128)S(1)}, u32[]{:S(2)}, u32[]{:S(2)}) collective-permute-start(f32[16,3072]{1,0:T(8,128)S(1)} %fusion), channel_id=1, source_target_pairs={{0,22},{1,23},{2,24},{3,25},{4,26},{5,27},{6,28},{7,29},{8,30},{9,... | collective-permute-start | bytes 589832
  629.5 28.1 %collective-permute-start.20 = (f32[16,3072]{1,0:T(8,128)S(1)}, f32[16,3072]{1,0:T(8,128)S(1)}, u32[]{:S(2)}, u32[]{:S(2)}) collective-permute-start(f32[16,3072]{1,0:T(8,128)S(1)} %fusion), channel_id=1, source_target_pairs={{0,21},{1,22},{2,23},{3,24},{4,25},{5,26},{6,27},{7,28},{8,29},{9,... | collective-permute-start | bytes 589832
  635.2 25.9 %collective-permute-start.19 = (f32[16,3072]{1,0:T(8,128)S(1)}, f32[16,3072]{1,0:T(8,128)}, u32[]{:S(2)}, u32[]{:S(2)}) collective-permute-start(f32[16,3072]{1,0:T(8,128)S(1)} %fusion), channel_id=1, source_target_pairs={{0,20},{1,21},{2,22},{3,23},{4,24},{5,25},{6,26},{7,27},{8,28},{9,... | collective-permute-start | bytes 589832
  653.6 23.0 %collective-permute-start.17 = (f32[16,3072]{1,0:T(8,128)S(1)}, f32[16,3072]{1,0:T(8,128)}, u32[]{:S(2)}, u32[]{:S(2)}) collective-permute-start(f32[16,3072]{1,0:T(8,128)S(1)} %fusion), channel_id=1, source_target_pairs={{0,18},{1,19},{2,20},{3,21},{4,22},{5,23},{6,24},{7,25},{8,26},{9,... | collective-permute-start | bytes 589832
  655.6 31.4 %collective-permute-start.16 = (f32[16,3072]{1,0:T(8,128)S(1)}, f32[16,3072]{1,0:T(8,128)}, u32[]{:S(2)}, u32[]{:S(2)}) collective-permute-start(f32[16,3072]{1,0:T(8,128)S(1)} %fusion), channel_id=1, source_target_pairs={{0,17},{1,18},{2,19},{3,20},{4,21},{5,22},{6,23},{7,24},{8,25},{9,... | collective-permute-start | bytes 589832
  657.6 44.1 %collective-permute-start.15 = (f32[16,3072]{1,0:T(8,128)S(1)}, f32[16,3072]{1,0:T(8,128)}, u32[]{:S(2)}, u32[]{:S(2)}) collective-permute-start(f32[16,3072]{1,0:T(8,128)S(1)} %fusion), channel_id=1, source_target_pairs={{0,16},{1,17},{2,18},{3,19},{4,20},{5,21},{6,22},{7,23},{8,24},{9,... | collective-permute-start | bytes 589832
  661.2 67.8 %collective-permute-start.14 = (f32[16,3072]{1,0:T(8,128)S(1)}, f32[16,3072]{1,0:T(8,128)S(1)}, u32[]{:S(2)}, u32[]{:S(2)}) collective-permute-start(f32[16,3072]{1,0:T(8,128)S(1)} %fusion), channel_id=1, source_target_pairs={{0,15},{1,16},{2,17},{3,18},{4,19},{5,20},{6,21},{7,22},{8,23},{9,... | collective-permute-start | bytes 589832
  664.5 65.8 %collective-permute-start.13 = (f32[16,3072]{1,0:T(8,128)S(1)}, f32[16,3072]{1,0:T(8,128)S(1)}, u32[]{:S(2)}, u32[]{:S(2)}) collective-permute-start(f32[16,3072]{1,0:T(8,128)S(1)} %fusion), channel_id=1, source_target_pairs={{0,14},{1,15},{2,16},{3,17},{4,18},{5,19},{6,20},{7,21},{8,22},{9,... | collective-permute-start | bytes 589832
  676.7 58.9 %collective-permute-start.12 = (f32[16,3072]{1,0:T(8,128)S(1)}, f32[16,3072]{1,0:T(8,128)S(1)}, u32[]{:S(2)}, u32[]{:S(2)}) collective-permute-start(f32[16,3072]{1,0:T(8,128)S(1)} %fusion), channel_id=1, source_target_pairs={{0,13},{1,14},{2,15},{3,16},{4,17},{5,18},{6,19},{7,20},{8,21},{9,... | collective-permute-start | bytes 589832
  687.0 50.5 %collective-permute-start.11 = (f32[16,3072]{1,0:T(8,128)S(1)}, f32[16,3072]{1,0:T(8,128)S(1)}, u32[]{:S(2)}, u32[]{:S(2)}) collective-permute-start(f32[16,3072]{1,0:T(8,128)S(1)} %fusion), channel_id=1, source_target_pairs={{0,12},{1,13},{2,14},{3,15},{4,16},{5,17},{6,18},{7,19},{8,20},{9,... | collective-permute-start | bytes 589832
  701.7 38.4 %collective-permute-start.10 = (f32[16,3072]{1,0:T(8,128)S(1)}, f32[16,3072]{1,0:T(8,128)S(1)}, u32[]{:S(2)}, u32[]{:S(2)}) collective-permute-start(f32[16,3072]{1,0:T(8,128)S(1)} %fusion), channel_id=1, source_target_pairs={{0,11},{1,12},{2,13},{3,14},{4,15},{5,16},{6,17},{7,18},{8,19},{9,... | collective-permute-start | bytes 589832
  729.0 23.7 %collective-permute-start.9 = (f32[16,3072]{1,0:T(8,128)S(1)}, f32[16,3072]{1,0:T(8,128)S(1)}, u32[]{:S(2)}, u32[]{:S(2)}) collective-permute-start(f32[16,3072]{1,0:T(8,128)S(1)} %fusion), channel_id=1, source_target_pairs={{0,10},{1,11},{2,12},{3,13},{4,14},{5,15},{6,16},{7,17},{8,18},{9,... | collective-permute-start | bytes 589832
  730.3 29.1 %collective-permute-start.8 = (f32[16,3072]{1,0:T(8,128)S(1)}, f32[16,3072]{1,0:T(8,128)S(1)}, u32[]{:S(2)}, u32[]{:S(2)}) collective-permute-start(f32[16,3072]{1,0:T(8,128)S(1)} %fusion), channel_id=1, source_target_pairs={{0,9},{1,10},{2,11},{3,12},{4,13},{5,14},{6,15},{7,16},{8,17},{9,1... | collective-permute-start | bytes 589832
  735.5 25.8 %collective-permute-start.7 = (f32[16,3072]{1,0:T(8,128)S(1)}, f32[16,3072]{1,0:T(8,128)S(1)}, u32[]{:S(2)}, u32[]{:S(2)}) collective-permute-start(f32[16,3072]{1,0:T(8,128)S(1)} %fusion), channel_id=1, source_target_pairs={{0,8},{1,9},{2,10},{3,11},{4,12},{5,13},{6,14},{7,15},{8,16},{9,17... | collective-permute-start | bytes 589832
  737.5 28.4 %collective-permute-start.6 = (f32[16,3072]{1,0:T(8,128)S(1)}, f32[16,3072]{1,0:T(8,128)S(1)}, u32[]{:S(2)}, u32[]{:S(2)}) collective-permute-start(f32[16,3072]{1,0:T(8,128)S(1)} %fusion), channel_id=1, source_target_pairs={{0,7},{1,8},{2,9},{3,10},{4,11},{5,12},{6,13},{7,14},{8,15},{9,16}... | collective-permute-start | bytes 589832
  740.8 27.1 %collective-permute-start.5 = (f32[16,3072]{1,0:T(8,128)S(1)}, f32[16,3072]{1,0:T(8,128)S(1)}, u32[]{:S(2)}, u32[]{:S(2)}) collective-permute-start(f32[16,3072]{1,0:T(8,128)S(1)} %fusion), channel_id=1, source_target_pairs={{0,6},{1,7},{2,8},{3,9},{4,10},{5,11},{6,12},{7,13},{8,14},{9,15},... | collective-permute-start | bytes 589832
  752.7 25.3 %collective-permute-start.4 = (f32[16,3072]{1,0:T(8,128)S(1)}, f32[16,3072]{1,0:T(8,128)}, u32[]{:S(2)}, u32[]{:S(2)}) collective-permute-start(f32[16,3072]{1,0:T(8,128)S(1)} %fusion), channel_id=1, source_target_pairs={{0,5},{1,6},{2,7},{3,8},{4,9},{5,10},{6,11},{7,12},{8,13},{9,14},{... | collective-permute-start | bytes 589832
  778.0 174.8 %all-gather.3.cloned.1.call-start = ((), (), s32[]{:S(2)}) async-start(), calls=%async_computation.2 | async-start | bytes 3342336 | tf_op jit(solution)/shard_map/all_gather | solution.py:112
  (75 other events, 3260.6 us)
Sparse Core Ops, SparseCore 0:
  778.1 145.1 all-reduce.6
Sparse Core Ops, SparseCore 1:
  864.6 45.1 all-gather.2
